TPU v7x, 128 devices: a whole 4x4x4 slice. The times are simulated.
128 devices in a mesh: blk: 8 (over z_lo, y), width: 16 (over z_hi, x, core).
Axes of the slice: x: 4, y: 4, z: 4 (z_hi: 2, z_lo: 2; z = z_hi * 2 + z_lo), core: 2. Of those that a mesh axis runs over, the one named last changes fastest.
Arguments:
- tokens: bfloat16 [4096, 4096], P('blk', 'width'), may hold values from -96 to 96
- gates: float32 [16, 8], P('blk'), may hold values from 0 to 1, as said below
- w_gate: bfloat16 [8, 4096, 7168], P(None, 'width', 'blk'), may hold values from -0.25 to 0.25
- w_up: bfloat16 [8, 4096, 7168], P(None, 'width', 'blk'), may hold values from -0.25 to 0.25
- w_down: bfloat16 [8, 7168, 4096], P(None, 'blk', 'width'), may hold values from -0.21875 to 0.21875
Outputs:
- mixed: bfloat16 [4096, 4096], P('blk', 'width')
Inputs may be any that keep to these rules, and one draw needn't show every extreme that they name: Each row of gates is the first 8 entries of a softmax over 16 experts: positive, summing to less than 1.
All inputs are finite; a program needn't handle non-finite values.
Results may differ from a plain program's by a relative error of at most 0.034.
Values may be sent and summed in bfloat16 or wider, within the bound.
A program may use at most 128 MiB of HBM per device.

v0:
```python
import jax
import jax.numpy as jnp
from jax import lax
from jax.sharding import PartitionSpec as P

SEG = 256


def merge_all(gates_all, w_gate, w_up, w_down):
    merged_gate = jnp.einsum(
        "se,edf->sdf", gates_all, w_gate, preferred_element_type=jnp.float32
    ).astype(jnp.bfloat16)
    merged_up = jnp.einsum(
        "se,edf->sdf", gates_all, w_up, preferred_element_type=jnp.float32
    ).astype(jnp.bfloat16)
    merged_down = jnp.einsum(
        "se,efd->sdf", gates_all, w_down, preferred_element_type=jnp.float32
    ).astype(jnp.bfloat16)
    return (merged_gate, merged_up, merged_down)


def width_total(gate_part, up_part):
    gate_sum, up_sum = (
        lax.psum_scatter(
            gate_part.astype(jnp.bfloat16), "width", scatter_dimension=1, tiled=True
        ).astype(jnp.float32),
        lax.psum_scatter(
            up_part.astype(jnp.bfloat16), "width", scatter_dimension=1, tiled=True
        ).astype(jnp.float32),
    )
    share = (jax.nn.silu(gate_sum) * up_sum).astype(jnp.bfloat16)
    return lax.all_gather(share, "width", axis=1, tiled=True)


def project_pair(seg_rows, merged_gate, merged_up):
    gate_part = jnp.einsum(
        "std,sdf->stf", seg_rows, merged_gate, preferred_element_type=jnp.float32
    )
    up_part = jnp.einsum("std,sdf->stf", seg_rows, merged_up, preferred_element_type=jnp.float32)
    return (gate_part, up_part)


def per_device(tokens, gates, w_gate, w_up, w_down):
    feat_cols = tokens.shape[1]
    gates_all = lax.all_gather(gates, "blk", axis=0, tiled=True)
    merged_gate, merged_up, merged_down = merge_all(gates_all, w_gate, w_up, w_down)
    gathered = lax.all_gather(tokens, "blk", axis=0, tiled=True)
    seg_rows = gathered.reshape(-1, SEG, feat_cols)
    gate_part, up_part = project_pair(seg_rows, merged_gate, merged_up)
    hidden = width_total(gate_part, up_part)
    count = tokens.shape[0] * lax.axis_size("blk")
    term = jnp.einsum("stf,sdf->std", hidden, merged_down, preferred_element_type=jnp.float32)
    return lax.psum_scatter(
        term.reshape(count, feat_cols).astype(jnp.bfloat16), "blk", scatter_dimension=0, tiled=True
    )


def solution(mesh):
    return jax.shard_map(
        per_device,
        mesh=mesh,
        in_specs=(
            P("blk", "width"),
            P("blk", None),
            P(None, "width", "blk"),
            P(None, "width", "blk"),
            P(None, "blk", "width"),
        ),
        out_specs=P("blk", "width"),
        check_vma=False,
    )
```

profile of v0, /device:TPU:8, one launch (start us, length us, event | category | flops | bytes accessed | tf_op | source)
XLA Modules:
  0.0 387.4 jit_solution(14190873027044199025)
XLA Ops:
  6.5 0.0 all-gather.4.cloned.1.call-start
  6.5 0.7 all-gather.4.cloned.1.call-update
  7.3 0.0 reduce-scatter.4.cloned.1.call-start
  7.3 0.7 bitcast_convert_fusion
  8.0 16.4 %all-gather = bf16[8,2,8]{2,1,0:T(2,128)(2,1)S(1)} all-gather(bf16[1,2,8]{2,1,0:T(2,128)(2,1)S(1)} %bitcast_convert_fusion), channel_id=1, replica_groups=mesh['blk'=8,'width'=16] {'blk'}, dimensions={0}, use_global_device_ids=true | all-gather | bytes 288 | tf_op jit(solution)/shard_map/all_gather | solution.py:45
  24.4 7.7 %fusion.13 = bf16[16,256,896]{2,0,1:T(8,128)(2,1)} fusion(bf16[16,8,1]{1,0,2:T(8,128)(2,1)S(1)} %bitcast.27, bf16[8,256,896]{2,1,0:T(8,128)(2,1)} %param.7), kind=kOutput, calls=%fused_computation.14 | convolution fusion | flops 58720256 | bytes 11010304 | tf_op jit(solution)/shard_map/se,edf->sdf/dot_general | solution.py:10
  32.0 11.9 %copy.10 = bf16[16,256,896]{1,2,0:T(8,128)(2,1)} copy(bf16[16,256,896]{2,0,1:T(8,128)(2,1)} %fusion.13) | data formatting | bytes 14680064 | tf_op jit(solution)/shard_map/se,edf->sdf/dot_general | solution.py:10
  43.9 6.7 %all-gather.4.cloned.1.call-done = bf16[4096,256]{1,0:T(8,128)(2,1)} async-done(((bf16[512,256]{1,0:T(8,128)(2,1)}), bf16[4096,256]{1,0:T(8,128)(2,1)}) %all-gather.4.cloned.1.call-update) | async-done | bytes 2097168 | tf_op jit(solution)/shard_map/all_gather | solution.py:47
  50.6 8.8 %convert_bitcast_fusion.1 = bf16[16,256,896]{1,2,0:T(8,128)(2,1)} fusion(bf16[16,256,256]{2,1,0:T(8,128)(2,1)} %bitcast.24, bf16[16,256,896]{1,2,0:T(8,128)(2,1)} %copy.10), kind=kOutput, calls=%fused_computation.7 | convolution fusion | flops 1882718208 | bytes 16777216 | tf_op jit(solution)/shard_map/std,sdf->stf/dot_general | solution.py:36
  59.4 11.8 %copy.7 = bf16[16,256,896]{2,0,1:T(8,128)(2,1)} copy(bf16[16,256,896]{1,2,0:T(8,128)(2,1)} %convert_bitcast_fusion.1) | data formatting | bytes 14680064 | tf_op jit(solution)/shard_map/convert_element_type | solution.py:25
  71.2 0.0 reduce-scatter.4.cloned.1.call-update
  71.2 0.0 copy-start
  71.2 0.2 reduce-scatter.6.cloned.1.call-start
  71.5 7.7 %fusion.11 = bf16[16,256,896]{2,0,1:T(8,128)(2,1)} fusion(bf16[16,8,1]{1,0,2:T(8,128)(2,1)S(1)} %bitcast.28, bf16[8,256,896]{2,1,0:T(8,128)(2,1)} %param.8), kind=kOutput, calls=%fused_computation.12 | convolution fusion | flops 58720256 | bytes 11010304 | tf_op jit(solution)/shard_map/se,edf->sdf/dot_general | solution.py:13
  79.2 0.0 copy-done
  79.2 9.7 %fusion = bf16[16,896,256]{2,1,0:T(8,128)(2,1)} fusion(bf16[16,256,256]{2,1,0:T(8,128)(2,1)S(1)} %bitcast.25, bf16[16,256,896]{2,0,1:T(8,128)(2,1)} %fusion.11), kind=kOutput, calls=%fused_computation.1 | convolution fusion | flops 1879048192 | bytes 16777216 | tf_op jit(solution)/shard_map/std,sdf->stf/dot_general | solution.py:39
  89.0 12.1 %copy.13 = bf16[16,896,256]{1,0,2:T(8,128)(2,1)} copy(bf16[16,896,256]{2,1,0:T(8,128)(2,1)} %fusion) | data formatting | bytes 14680064 | tf_op jit(solution)/shard_map/std,sdf->stf/dot_general | solution.py:39
  101.1 0.0 reduce-scatter.6.cloned.1.call-update
  101.1 0.0 all-gather.6.cloned.1.call-start
  101.2 66.0 %reduce-scatter.4.cloned.1.call-done = bf16[16,16,896]{2,0,1:T(8,128)(2,1)} async-done(((bf16[16,256,896]{2,0,1:T(8,128)(2,1)}), bf16[16,16,896]{2,0,1:T(8,128)(2,1)}) %reduce-scatter.4.cloned.1.call-update) | async-done | bytes 458768 | tf_op jit(solution)/shard_map/reduce_scatter | solution.py:24
  167.1 97.7 %reduce-scatter.6.cloned.1.call-done = bf16[16,16,896]{2,0,1:T(8,128)(2,1)} async-done(((bf16[16,256,896]{2,0,1:T(8,128)(2,1)}), bf16[16,16,896]{2,0,1:T(8,128)(2,1)}) %reduce-scatter.6.cloned.1.call-update) | async-done | bytes 458768 | tf_op jit(solution)/shard_map/reduce_scatter | solution.py:27
  264.8 2.2 fusion.24
  267.1 0.0 all-gather.6.cloned.1.call-update
  267.1 0.3 reduce-scatter.8.cloned.1.call-start
  267.4 7.7 %fusion.9 = bf16[896,256,16]{1,2,0:T(8,128)(2,1)} fusion(bf16[16,8,1]{1,0,2:T(8,128)(2,1)S(1)} %bitcast.29, bf16[8,896,256]{2,1,0:T(8,128)(2,1)} %param.9), kind=kOutput, calls=%fused_computation.10 | convolution fusion | flops 58720256 | bytes 11010304 | tf_op jit(solution)/shard_map/se,efd->sdf/dot_general | solution.py:16
  275.0 11.7 %copy.15 = bf16[896,256,16]{0,1,2:T(8,128)(2,1)} copy(bf16[896,256,16]{1,2,0:T(8,128)(2,1)} %fusion.9) | data formatting | bytes 14680064 | tf_op jit(solution)/shard_map/se,efd->sdf/dot_general | solution.py:16
  286.7 47.8 %all-gather.6.cloned.1.call-done = bf16[16,256,896]{2,0,1:T(8,128)(2,1)} async-done(((bf16[16,16,896]{2,0,1:T(8,128)(2,1)}), bf16[16,256,896]{2,0,1:T(8,128)(2,1)}) %all-gather.6.cloned.1.call-update) | async-done | bytes 7340048 | tf_op jit(solution)/shard_map/all_gather | solution.py:32
  334.5 8.9 %fusion.15 = bf16[16,256,256]{2,1,0:T(8,128)(2,1)} fusion(bf16[896,256,16]{0,1,2:T(8,128)(2,1)} %copy.15, bf16[16,256,896]{2,0,1:T(8,128)(2,1)} %all-gather.6.cloned.1.call-done), kind=kOutput, calls=%fused_computation.16 | convolution fusion | flops 1880096768 | bytes 16777216 | tf_op jit(solution)/shard_map/stf,sdf->std/dot_general | solution.py:52
  343.3 0.0 reduce-scatter.8.cloned.1.call-update
  343.4 37.6 %reduce-scatter.8.cloned.1.call-done = bf16[512,256]{1,0:T(8,128)(2,1)} async-done(((bf16[4096,256]{1,0:T(8,128)(2,1)}), bf16[512,256]{1,0:T(8,128)(2,1)}) %reduce-scatter.8.cloned.1.call-update) | async-done | bytes 262160 | tf_op jit(solution)/shard_map/reduce_scatter | solution.py:53
Async XLA Ops:
  6.5 44.1 %all-gather.4.cloned.1.call-start = ((), (), s32[]{:S(2)}) async-start(), calls=%async_computation.3 | async-start | bytes 2359296 | tf_op jit(solution)/shard_map/all_gather | solution.py:47
  7.3 159.9 %reduce-scatter.4.cloned.1.call-start = ((), (), s32[]{:S(2)}) async-start(), calls=%async_computation.4 | async-start | bytes 7798784 | tf_op jit(solution)/shard_map/reduce_scatter | solution.py:24
  71.2 8.0 %copy-start = (bf16[4096,256]{1,0:T(8,128)(2,1)S(1)}, bf16[4096,256]{1,0:T(8,128)(2,1)}, u32[]{:S(2)}) copy-start(bf16[4096,256]{1,0:T(8,128)(2,1)} %all-gather.4.cloned.1.call-done) | copy-start | bytes 6291460
  71.2 193.6 %reduce-scatter.6.cloned.1.call-start = ((), (), s32[]{:S(2)}) async-start(), calls=%async_computation.5 | async-start | bytes 7798784 | tf_op jit(solution)/shard_map/reduce_scatter | solution.py:27
  101.1 233.4 %all-gather.6.cloned.1.call-start = ((), (), s32[]{:S(2)}) async-start(), calls=%async_computation.6 | async-start | bytes 7798784 | tf_op jit(solution)/shard_map/all_gather | solution.py:32
  267.1 113.8 %reduce-scatter.8.cloned.1.call-start = ((), (), s32[]{:S(2)}) async-start(), calls=%async_computation.7 | async-start | bytes 2359296 | tf_op jit(solution)/shard_map/reduce_scatter | solution.py:53
Sparse Core Ops, SparseCore 0:
  9.0 41.5 all-gather.3
  71.3 95.7 reduce-scatter.3
  171.9 92.8 reduce-scatter.5
  267.2 67.2 all-gather.5
  343.5 37.3 reduce-scatter.7
where the time goes:
time: 392 us; the launch traced here: 387 us
  waiting for transfers between devices  256 us (65%)
  matrix products  50.5 us (13%)
  local copies, waits for them, and re-layouts  47.5 us (12%)
  blocking collectives  16.4 us (4%)
  between operations  13.2 us (3%)
    reduce_scatter x1, waiting for transfers between devices, width_total(): lax.psum_scatter(up_part.astype(jnp.bfloat16), 'width', scatter_dimension...  97.7 us
    reduce_scatter x1, waiting for transfers between devices, width_total(): lax.psum_scatter(gate_part.astype(jnp.bfloat16), 'width', scatter_dimensi...  66 us
    all_gather x1, waiting for transfers between devices, width_total(): return lax.all_gather(share, 'width', axis=1, tiled=True)  47.8 us
    reduce_scatter x1, waiting for transfers between devices, per_device(): lax.psum_scatter(term.reshape(count, feat_cols).astype(jnp.bfloat16), 'bl...  37.6 us
    all_gather x1, blocking collectives, per_device(): gates_all = lax.all_gather(gates, 'blk', axis=0, tiled=True)  16.4 us
    dot_general x1, local copies, waits for them, and re-layouts, project_pair(): jnp.einsum('std,sdf->stf', seg_rows, merged_up, preferred_element_type=jn...  12.1 us
    dot_general x1, local copies, waits for them, and re-layouts, merge_all(): jnp.einsum('se,edf->sdf', gates_all, w_gate, preferred_element_type=jnp.f...  11.9 us
    convert_element_type x1, local copies, waits for them, and re-layouts, width_total(): gate_part.astype(jnp.bfloat16)  11.8 us
  transfers between devices with their start and end apart: 5, of which 5 were waited for; matrix products, arithmetic and copies ran while one was open for 18% of the time, Pallas kernels for 0%

commit v1 on v0

v1 whole, which is shorter than its diff:
```python
import functools
import jax
import jax.numpy as jnp
from jax import lax
from jax.experimental import pallas as pl
from jax.experimental.pallas import tpu as pltpu
from jax.sharding import PartitionSpec as P

SEG = 256
EXPERTS = 8
UNITS = 16
SUB = 32
TILE = 256
SLOTS = 4
MESH = pl.DeviceIdType.MESH
OFFSETS = (0, 1, 6, 9, 12, 15, 18, 22, 23)


def kernel(
    gates_ref, tokens_ref, wg_ref, wu_ref, wd_ref, out_ref,
    gbuf, kmat, keep, psend, precv, r1, r2, r3, merged, wdn, tok, hid, term, yrecv, zsend, zrecv,
    w_sem, l_sem, g_s, g_r, tok_s, tok_r, rs_s, rs_r, ag_s, ag_r, t_s, t_r, z_s, z_r,
):
    depth = tokens_ref.shape[1]
    ff = wg_ref.shape[2]
    cols = 2 * ff
    half, quarter, eighth, share = SEG // 2, SEG // 4, SEG // 8, SEG // 16

    w = lax.axis_index("width")
    b = lax.axis_index("blk")
    core = lax.rem(w, 2)
    x = lax.rem(w // 2, 4)
    zh = w // 8
    y = lax.rem(b, 4)
    zl = b // 4

    bit_a, bit_b = lax.rem((x + 1) // 2, 2), x // 2
    w_pair = w + 1 - 2 * core
    w_a = (zh * 4 + x + 1 - 2 * lax.rem(x, 2)) * 2 + core
    w_b = (zh * 4 + 3 - x) * 2 + core
    w_z = ((1 - zh) * 4 + x) * 2 + core
    b_z = (1 - zl) * 4 + y

    def mul(value, by):
        return pl.multiple_of(value, by)

    def dim(u, place):
        d = lax.rem(u + place, 3)
        e0, e1, e2 = (2 - d) * (1 - d) // 2, d * (2 - d), d * (d - 1) // 2
        return e0 * bit_a + e1 * bit_b + e2 * zh, e0 * w_a + e1 * w_b + e2 * w_z

    def place_of(u):
        r, j = u // 2, lax.rem(u, 2)
        q = lax.rem(r, 4)
        dy = lax.rem(1 + 2 * q + q // 2, 4)
        dz = lax.rem((r + 1) // 4, 2)
        zo = zl + dz - 2 * zl * dz
        owner = zo * 4 + lax.rem(y + dy, 4)
        return dy, owner, owner * 2 + j

    def rcopy(src, dst, send, recv, device):
        return pltpu.make_async_remote_copy(
            src_ref=src, dst_ref=dst, send_sem=send, recv_sem=recv, device_id=device, device_id_type=MESH
        )

    def weight_copies(i):
        rows = pl.ds(mul(i * SUB, SUB), SUB)
        return (
            pltpu.make_async_copy(wg_ref.at[:, rows, :], keep.at[:, rows, pl.ds(0, ff)], w_sem.at[0, i]),
            pltpu.make_async_copy(wu_ref.at[:, rows, :], keep.at[:, rows, pl.ds(ff, ff)], w_sem.at[1, i]),
        )

    own_tok = [
        pltpu.make_async_copy(tokens_ref.at[pl.ds(j * SEG, SEG), :], tok.at[2 * b + j], l_sem.at[j])
        for j in range(2)
    ]
    down_copy = pltpu.make_async_copy(wd_ref, wdn, l_sem.at[2])

    for copy in own_tok:
        copy.start()

    @pl.loop(0, depth // SUB)
    def _(i):
        for copy in weight_copies(i):
            copy.start()

    down_copy.start()

    gbuf[b] = jnp.zeros((8, 128), jnp.float32)
    gbuf[b, 0:2, 0:EXPERTS] = gates_ref[...]

    barrier = pltpu.get_barrier_semaphore()
    for partner in (w_pair, w_a, w_b, w_z):
        pl.semaphore_signal(barrier, inc=1, device_id=(b, partner), device_id_type=MESH)
    for p in range(1, 8):
        pl.semaphore_signal(barrier, inc=1, device_id=(lax.rem(b + p, 8), w), device_id_type=MESH)
    pl.semaphore_wait(barrier, 11)

    def gate_copy(p):
        return rcopy(gbuf.at[b], gbuf.at[b], g_s.at[p], g_r.at[p], (lax.rem(b + p, 8), w))

    def gate_arrival(p):
        src = lax.rem(b + 8 - p, 8)
        return rcopy(gbuf.at[src], gbuf.at[src], g_s.at[p], g_r.at[p], (lax.rem(b + p, 8), w))

    for p in range(1, 8):
        gate_copy(p).start()

    def tok_copy(k, source, target):
        block = tok.at[pl.ds(2 * source, 2)]
        return rcopy(block, block, tok_s.at[k], tok_r.at[source], (target, w))

    def y_block(dy):
        return zl * 4 + lax.rem(y + dy, 4)

    for copy in own_tok:
        copy.wait()
    tok_copy(0, b, b_z).start()
    for k, dy in enumerate((3, 1, 2)):
        tok_copy(1 + k, b, y_block(dy)).start()

    for p in range(1, 8):
        gate_arrival(p).wait_recv()
    rows_k, cols_k = UNITS * SUB, EXPERTS * SUB
    shift = SUB.bit_length() - 1
    row = lax.broadcasted_iota(jnp.int32, (rows_k, 64), 0) >> shift
    col = lax.broadcasted_iota(jnp.int32, (rows_k, 64), 1)
    pick_row = ((row >> 1) * 8 + (row & 1) == col).astype(jnp.float32).astype(jnp.bfloat16)
    pick_col = (
        (lax.broadcasted_iota(jnp.int32, (128, cols_k), 1) >> shift)
        == lax.broadcasted_iota(jnp.int32, (128, cols_k), 0)
    ).astype(jnp.float32).astype(jnp.bfloat16)
    weights = gbuf[...].reshape(64, 128).astype(jnp.bfloat16)
    spread = jnp.dot(pick_row, weights, preferred_element_type=jnp.float32).astype(jnp.bfloat16)
    spread = jnp.dot(spread, pick_col, preferred_element_type=jnp.float32)
    same = (lax.broadcasted_iota(jnp.int32, (rows_k, cols_k), 0) & (SUB - 1)) == (
        lax.broadcasted_iota(jnp.int32, (rows_k, cols_k), 1) & (SUB - 1)
    )
    kmat[...] = jnp.where(same, spread, 0.0).astype(jnp.bfloat16)

    @pl.loop(0, depth // SUB)
    def _(i):
        for copy in weight_copies(i):
            copy.wait()
        rows = pl.ds(mul(i * SUB, SUB), SUB)
        for n in range(cols // TILE):
            experts = keep[:, rows, n * TILE : (n + 1) * TILE].reshape(cols_k, TILE)
            total = jnp.dot(kmat[...], experts, preferred_element_type=jnp.float32)
            merged[:, n, rows, :] = total.astype(jnp.bfloat16).reshape(UNITS, SUB, TILE)

    tok_copy(0, b_z, b_z).wait_recv()
    for k, dy in enumerate((3, 1, 2)):
        tok_copy(4 + k, b_z, y_block(dy)).start()

    def kept(u, offset, count):
        return keep.at[u // 2, pl.ds(mul(lax.rem(u, 2) * half + offset, 16), count), :]

    def reduce_copy(u, stage):
        if stage == 0:
            return rcopy(psend.at[lax.rem(u, SLOTS)], precv.at[u], rs_s.at[0, u], rs_r.at[0, u], (b, w_pair))
        (b1, w1), (b2, w2), (b3, w3) = (dim(u, k) for k in range(3))
        if stage == 1:
            return rcopy(kept(u, (1 - b1) * quarter, quarter), r1.at[u], rs_s.at[1, u], rs_r.at[1, u], (b, w1))
        if stage == 2:
            offset = b1 * quarter + (1 - b2) * eighth
            return rcopy(kept(u, offset, eighth), r2.at[u], rs_s.at[2, u], rs_r.at[2, u], (b, w2))
        offset = b1 * quarter + b2 * eighth + (1 - b3) * share
        return rcopy(kept(u, offset, share), r3.at[u], rs_s.at[3, u], rs_r.at[3, u], (b, w3))

    def gather_copy(u, stage):
        (b1, w1), (b2, w2), (b3, w3) = (dim(u, k) for k in range(3))
        offset = core * half
        if stage < 3:
            offset = offset + b1 * quarter
        if stage < 2:
            offset = offset + b2 * eighth
        if stage < 1:
            offset = offset + b3 * share
        count = share << stage
        block = hid.at[u, pl.ds(mul(offset, 16), count), :]
        target = (w3, w2, w1, w_pair)[stage]
        return rcopy(block, block, ag_s.at[stage, u], ag_r.at[stage, u], (b, target))

    def gather_arrival(u, stage):
        (b1, w1), (b2, w2), (b3, w3) = (dim(u, k) for k in range(3))
        offset = core * half if stage < 3 else (1 - core) * half
        if stage < 3:
            offset = offset + (b1 if stage < 2 else 1 - b1) * quarter
        if stage < 2:
            offset = offset + (b2 if stage < 1 else 1 - b2) * eighth
        if stage < 1:
            offset = offset + (1 - b3) * share
        count = share << stage
        block = hid.at[u, pl.ds(mul(offset, 16), count), :]
        target = (w3, w2, w1, w_pair)[stage]
        return rcopy(block, block, ag_s.at[stage, u], ag_r.at[stage, u], (b, target))

    def term_copy(u):
        dy, owner, _ = place_of(u)
        return rcopy(term.at[u], yrecv.at[u], t_s.at[u], t_r.at[u], (y_block(dy), w))

    def f32(block):
        return block.astype(jnp.float32)

    def project(u):
        _, owner, s = place_of(u)

        @pl.when((lax.rem(u, 2) == 0) & (u != 6) & (u != 14))
        def _():
            tok_copy(0, owner, b_z).wait_recv()

        @pl.when(u >= SLOTS)
        def _():
            reduce_copy(u - SLOTS, 0).wait_send()

        rows = jnp.concatenate(
            [tok[s, pl.ds(mul(core * half, half), half), :], tok[s, pl.ds(mul((1 - core) * half, half), half), :]],
            axis=0,
        )
        slot = lax.rem(u, SLOTS)
        mine = pl.ds(mul(lax.rem(u, 2) * half, half), half)
        for n in range(cols // TILE):
            part = jnp.dot(rows, merged[s, n], preferred_element_type=jnp.float32).astype(jnp.bfloat16)
            keep[u // 2, mine, n * TILE : (n + 1) * TILE] = part[:half]
            psend[slot, :, n * TILE : (n + 1) * TILE] = part[half:]
        reduce_copy(u, 0).start()

    def reduce_1(u):
        reduce_copy(u, 0).wait_recv()
        b1, _ = dim(u, 0)
        base = lax.rem(u, 2) * half
        for i in range(quarter // 16):
            offset = (1 - b1) * quarter + i * 16
            at = pl.ds(mul(base + offset, 16), 16)
            total = f32(keep[u // 2, at, :]) + f32(precv[u, pl.ds(mul(offset, 16), 16), :])
            keep[u // 2, at, :] = total.astype(jnp.bfloat16)
        reduce_copy(u, 1).start()

    def reduce_2(u):
        reduce_copy(u, 1).wait_recv()
        (b1, _), (b2, _) = dim(u, 0), dim(u, 1)
        base = lax.rem(u, 2) * half
        for i in range(eighth // 16):
            inner = (1 - b2) * eighth + i * 16
            offset = b1 * quarter + inner
            at = pl.ds(mul(base + offset, 16), 16)
            total = (
                f32(keep[u // 2, at, :])
                + f32(precv[u, pl.ds(mul(offset, 16), 16), :])
                + f32(r1[u, pl.ds(mul(inner, 16), 16), :])
            )
            keep[u // 2, at, :] = total.astype(jnp.bfloat16)
        reduce_copy(u, 2).start()

    def gathered(u, last):
        (b1, _), (b2, _) = dim(u, 0), dim(u, 1)
        base = lax.rem(u, 2) * half
        inner = b2 * eighth + last * share
        offset = b1 * quarter + inner
        return pl.ds(mul(base + offset, 16), 16), (
            f32(keep[u // 2, pl.ds(mul(base + offset, 16), 16), :])
            + f32(precv[u, pl.ds(mul(offset, 16), 16), :])
            + f32(r1[u, pl.ds(mul(inner, 16), 16), :])
            + f32(r2[u, pl.ds(mul(last * share, 16), 16), :])
        )

    def reduce_3(u):
        reduce_copy(u, 2).wait_recv()
        b3, _ = dim(u, 2)
        at, total = gathered(u, 1 - b3)
        keep[u // 2, at, :] = total.astype(jnp.bfloat16)
        reduce_copy(u, 3).start()

    def activate(u):
        reduce_copy(u, 3).wait_recv()
        (b1, _), (b2, _), (b3, _) = (dim(u, k) for k in range(3))
        _, total = gathered(u, b3)
        total = total + f32(r3[u])
        gate, up = total[:, :ff], total[:, ff:]
        value = (gate / (1.0 + jnp.exp(-gate)) * up).astype(jnp.bfloat16)
        offset = core * half + b1 * quarter + b2 * eighth + b3 * share
        hid[u, pl.ds(mul(offset, 16), 16), :] = value
        gather_copy(u, 0).start()

    def spread_on(stage):
        def run(u):
            gather_arrival(u, stage - 1).wait_recv()
            gather_copy(u, stage).start()

        return run

    def finish(u):
        gather_arrival(u, 3).wait_recv()
        dy, _, s = place_of(u)
        down = merged[s, 0:4].reshape(4 * TILE, TILE)[:ff]
        part = jnp.dot(hid[u], down, preferred_element_type=jnp.float32)
        term[u] = part.astype(jnp.bfloat16)

        @pl.when(dy != 0)
        def _():
            term_copy(u).start()

    def merge_down(i):
        rows = pl.ds(mul(i * SUB, SUB), SUB)
        experts = wdn[:, rows, :].reshape(cols_k, TILE)
        total = jnp.dot(kmat[...], experts, preferred_element_type=jnp.float32)
        to = pl.ds(mul(lax.rem(i, TILE // SUB) * SUB, SUB), SUB)
        merged[:, i // (TILE // SUB), to, :] = total.astype(jnp.bfloat16).reshape(UNITS, SUB, TILE)

    def z_copy(j):
        return rcopy(zsend.at[j], zrecv.at[j], z_s.at[j], z_r.at[j], (b_z, w))

    def send_z():
        for j in range(2):
            total = f32(term[6 + j])
            for r in (4, 5, 6):
                term_copy(2 * r + j).wait_recv()
                total = total + f32(yrecv[2 * r + j])
            zsend[j] = total.astype(jnp.bfloat16)
            z_copy(j).start()

    stages = (
        project, reduce_1, reduce_2, reduce_3, activate,
        spread_on(1), spread_on(2), spread_on(3), finish,
    )
    down_steps = OFFSETS[8] - UNITS
    per_step = -(-(ff // SUB) // down_steps)

    @pl.loop(0, UNITS + OFFSETS[8])
    def _(t):
        for stage, offset in zip(stages, OFFSETS):
            @pl.when((t >= offset) & (t < offset + UNITS))
            def _():
                stage(t - offset)

        @pl.when(t == UNITS)
        def _():
            down_copy.wait()

        @pl.when((t >= UNITS) & (t < OFFSETS[8]))
        def _():
            @pl.loop(0, per_step)
            def _(k):
                i = (t - UNITS) * per_step + k

                @pl.when(i < ff // SUB)
                def _():
                    merge_down(i)

        @pl.when(t == OFFSETS[8] + 14)
        def _():
            send_z()

    for j in range(2):
        total = f32(term[14 + j])
        for r in (0, 1, 2):
            term_copy(2 * r + j).wait_recv()
            total = total + f32(yrecv[2 * r + j])
        z_copy(j).wait_recv()
        total = total + f32(zrecv[j])
        out_ref[j * SEG : (j + 1) * SEG, :] = total.astype(jnp.bfloat16)

    for p in range(1, 8):
        gate_copy(p).wait_send()
    tok_copy(0, b, b_z).wait_send()
    for k, dy in enumerate((3, 1, 2)):
        tok_copy(1 + k, b, y_block(dy)).wait_send()
        tok_copy(4 + k, b_z, y_block(dy)).wait_send()

    @pl.loop(0, UNITS)
    def _(u):
        @pl.when(u >= UNITS - SLOTS)
        def _():
            reduce_copy(u, 0).wait_send()

        for stage in (1, 2, 3):
            reduce_copy(u, stage).wait_send()
        for stage in range(4):
            gather_copy(u, stage).wait_send()

        @pl.when((u // 2 != 3) & (u // 2 != 7))
        def _():
            term_copy(u).wait_send()

    for j in range(2):
        z_copy(j).wait_send()


def per_device(tokens, gates, w_gate, w_up, w_down):
    depth = tokens.shape[1]
    ff = w_gate.shape[2]
    cols = 2 * ff
    half = SEG // 2
    bf16 = jnp.bfloat16
    anywhere = pl.BlockSpec(memory_space=pl.ANY)
    vmem = pl.BlockSpec(memory_space=pltpu.VMEM)
    dma = pltpu.SemaphoreType.DMA
    return pl.pallas_call(
        kernel,
        out_shape=jax.ShapeDtypeStruct(tokens.shape, bf16),
        in_specs=[vmem, anywhere, anywhere, anywhere, anywhere],
        out_specs=vmem,
        scratch_shapes=[
            pltpu.VMEM((8, 8, 128), jnp.float32),
            pltpu.VMEM((UNITS * SUB, EXPERTS * SUB), bf16),
            pltpu.VMEM((EXPERTS, depth, cols), bf16),
            pltpu.VMEM((SLOTS, half, cols), bf16),
            pltpu.VMEM((UNITS, half, cols), bf16),
            pltpu.VMEM((UNITS, half // 2, cols), bf16),
            pltpu.VMEM((UNITS, half // 4, cols), bf16),
            pltpu.VMEM((UNITS, half // 8, cols), bf16),
            pltpu.VMEM((UNITS, cols // TILE, depth, TILE), bf16),
            pltpu.VMEM(w_down.shape, bf16),
            pltpu.VMEM((UNITS, SEG, depth), bf16),
            pltpu.VMEM((UNITS, SEG, ff), bf16),
            pltpu.VMEM((UNITS, SEG, depth), bf16),
            pltpu.VMEM((UNITS, SEG, depth), bf16),
            pltpu.VMEM((2, SEG, depth), bf16),
            pltpu.VMEM((2, SEG, depth), bf16),
            dma((2, depth // SUB)),
            dma((3,)),
            dma((8,)),
            dma((8,)),
            dma((8,)),
            dma((8,)),
            dma((4, UNITS)),
            dma((4, UNITS)),
            dma((4, UNITS)),
            dma((4, UNITS)),
            dma((UNITS,)),
            dma((UNITS,)),
            dma((2,)),
            dma((2,)),
        ],
        compiler_params=pltpu.CompilerParams(
            collective_id=0, has_side_effects=True, vmem_limit_bytes=61 * 2**20
        ),
        cost_estimate=pl.CostEstimate(flops=2 * 2**33, bytes_accessed=12 * 2**20, transcendentals=0),
    )(gates, tokens, w_gate, w_up, w_down)


def solution(mesh):
    return jax.shard_map(
        per_device,
        mesh=mesh,
        in_specs=(
            P("blk", "width"),
            P("blk", None),
            P(None, "width", "blk"),
            P(None, "width", "blk"),
            P(None, "blk", "width"),
        ),
        out_specs=P("blk", "width"),
        check_vma=False,
    )
```

time: 392 us -> 113 us (0.29); the launches traced: 387 us -> 113 us
  waiting for transfers between devices: 256 us -> 0 us
  Pallas kernels: 0 us -> 112 us
  matrix products: 50.5 us -> 0 us
  local copies, waits for them, and re-layouts: 47.5 us -> 1.67 us
  blocking collectives: 16.4 us -> 0 us
  between operations: 13.2 us -> 0.01 us
    reduce_scatter x3 -> x0, waiting for transfers between devices: 201 us -> none  [the longest x1 97.7 us: width_total(): lax.psum_scatter(up_part.astype(jnp.bfloat16), 'width', scatter_dimension...]
    pallas_call x0 -> x1, Pallas kernels: none -> 112 us  [per_device(): pl.pallas_call(kernel, out_shape=jax.ShapeDtypeStruct(tokens.shape, bf16)...]
    all_gather x2 -> x0, waiting for transfers between devices: 54.5 us -> none  [the longest x1 47.8 us: width_total(): return lax.all_gather(share, 'width', axis=1, tiled=True)]
    dot_general x6 -> x0, matrix products: 50.5 us -> none  [the longest x1 9.75 us: project_pair(): jnp.einsum('std,sdf->stf', seg_rows, merged_up, preferred_element_type=jn...]
    dot_general x3 -> x0, local copies, waits for them, and re-layouts: 35.7 us -> none  [the longest x1 12.1 us: project_pair(): jnp.einsum('std,sdf->stf', seg_rows, merged_up, preferred_element_type=jn...]
    all_gather x1 -> x0, blocking collectives: 16.4 us -> none  [per_device(): gates_all = lax.all_gather(gates, 'blk', axis=0, tiled=True)]
    convert_element_type x1 -> x0, local copies, waits for them, and re-layouts: 11.8 us -> none  [width_total(): gate_part.astype(jnp.bfloat16)]
  transfers between devices with their start and end apart: 5 -> 0, of which waited for: 5 -> 0; matrix products, arithmetic and copies ran while one was open for 18% -> 0% of each run, Pallas kernels for 0% -> 0%
where the time goes in v1:
time: 113 us
  Pallas kernels  112 us (99%)
  local copies, waits for them, and re-layouts  1.67 us (1%)
    pallas_call x1, Pallas kernels, per_device(): pl.pallas_call(kernel, out_shape=jax.ShapeDtypeStruct(tokens.shape, bf16)...  112 us

profile of v1, /device:TPU:8, one launch (start us, length us, event | category | flops | bytes accessed | tf_op | source)
XLA Modules:
  0.0 113.2 jit_solution(9516342651624809357)
XLA Ops:
  0.0 111.5 %shard_map.55 = bf16[512,256]{1,0:T(8,128)(2,1)} custom-call(f32[2,8]{1,0:T(2,128)} %gates_ref.1, bf16[512,256]{1,0:T(8,128)(2,1)} %tokens_ref.1, bf16[8,256,896]{2,1,0:T(8,128)(2,1)} %wg_ref.1, bf16[8,256,896]{2,1,0:T(8,128)(2,1)} %wu_ref.1, bf16[8,896,256]{2,1,0:T(8,128)(2,1)} %wd_ref.1), custom_call_target="tpu_custom_call" | custom-call | flops 17179869184 | bytes 12582912 | tf_op jit(solution)/shard_map/pallas_call | solution.py:398
  111.5 1.7 %copy.7 = bf16[512,256]{1,0:T(8,128)(2,1)} copy(bf16[512,256]{1,0:T(8,128)(2,1)} %shard_map.55) | data formatting | bytes 524288

commit v2 on v1

--- a/solution.py
+++ b/solution.py
@@ -13,7 +13,7 @@
 TILE = 256
 SLOTS = 4
 MESH = pl.DeviceIdType.MESH
-OFFSETS = (0, 1, 6, 9, 12, 15, 18, 22, 23)
+OFFSETS = (0, 1, 6, 9, 12, 15, 18, 20, 21)
 
 
 def kernel(
@@ -52,7 +52,7 @@
     def place_of(u):
         r, j = u // 2, lax.rem(u, 2)
         q = lax.rem(r, 4)
-        dy = lax.rem(1 + 2 * q + q // 2, 4)
+        dy = lax.rem(2 + 3 * q + 3 * (q // 2) + 2 * (q // 3), 4)
         dz = lax.rem((r + 1) // 4, 2)
         zo = zl + dz - 2 * zl * dz
         owner = zo * 4 + lax.rem(y + dy, 4)
@@ -116,7 +116,7 @@
     for copy in own_tok:
         copy.wait()
     tok_copy(0, b, b_z).start()
-    for k, dy in enumerate((3, 1, 2)):
+    for k, dy in enumerate((2, 3, 1)):
         tok_copy(1 + k, b, y_block(dy)).start()
 
     for p in range(1, 8):
@@ -148,9 +148,11 @@
             total = jnp.dot(kmat[...], experts, preferred_element_type=jnp.float32)
             merged[:, n, rows, :] = total.astype(jnp.bfloat16).reshape(UNITS, SUB, TILE)
 
-    tok_copy(0, b_z, b_z).wait_recv()
-    for k, dy in enumerate((3, 1, 2)):
-        tok_copy(4 + k, b_z, y_block(dy)).start()
+        @pl.when(i == 2)
+        def _():
+            tok_copy(0, b_z, b_z).wait_recv()
+            for k, dy in enumerate((2, 3, 1)):
+                tok_copy(4 + k, b_z, y_block(dy)).start()
 
     def kept(u, offset, count):
         return keep.at[u // 2, pl.ds(mul(lax.rem(u, 2) * half + offset, 16), count), :]
@@ -196,8 +198,13 @@
         return rcopy(block, block, ag_s.at[stage, u], ag_r.at[stage, u], (b, target))
 
     def term_copy(u):
-        dy, owner, _ = place_of(u)
-        return rcopy(term.at[u], yrecv.at[u], t_s.at[u], t_r.at[u], (y_block(dy), w))
+        dy, _, _ = place_of(u)
+        return rcopy(term.at[u], yrecv.at[u], t_s.at[0, u], t_r.at[0, u], (y_block(dy), w))
+
+    def relay_copy(u, side):
+        rows = pl.ds(side * half, half)
+        to = (y_block(1 + 2 * side), w)
+        return rcopy(term.at[u, rows, :], yrecv.at[u, rows, :], t_s.at[side, u], t_r.at[side, u], to)
 
     def f32(block):
         return block.astype(jnp.float32)
@@ -296,9 +303,20 @@
         part = jnp.dot(hid[u], down, preferred_element_type=jnp.float32)
         term[u] = part.astype(jnp.bfloat16)
 
-        @pl.when(dy != 0)
-        def _():
-            term_copy(u).start()
+        @pl.when(dy == 2)
+        def _():
+            for side in range(2):
+                relay_copy(u, side).start()
+
+        for side in range(2):
+            @pl.when(dy == 1 + 2 * side)
+            def _():
+                far = u - 2 - 2 * side
+                relay_copy(far, side).wait_recv()
+                rows = pl.ds(side * half, half)
+                total = part[side * half : (side + 1) * half] + f32(yrecv[far, rows, :])
+                term[u, rows, :] = total.astype(jnp.bfloat16)
+                term_copy(u).start()
 
     def merge_down(i):
         rows = pl.ds(mul(i * SUB, SUB), SUB)
@@ -313,7 +331,7 @@
     def send_z():
         for j in range(2):
             total = f32(term[6 + j])
-            for r in (4, 5, 6):
+            for r in (5, 6):
                 term_copy(2 * r + j).wait_recv()
                 total = total + f32(yrecv[2 * r + j])
             zsend[j] = total.astype(jnp.bfloat16)
@@ -347,13 +365,11 @@
                 def _():
                     merge_down(i)
 
-        @pl.when(t == OFFSETS[8] + 14)
-        def _():
-            send_z()
+    send_z()
 
     for j in range(2):
         total = f32(term[14 + j])
-        for r in (0, 1, 2):
+        for r in (1, 2):
             term_copy(2 * r + j).wait_recv()
             total = total + f32(yrecv[2 * r + j])
         z_copy(j).wait_recv()
@@ -363,7 +379,7 @@
     for p in range(1, 8):
         gate_copy(p).wait_send()
     tok_copy(0, b, b_z).wait_send()
-    for k, dy in enumerate((3, 1, 2)):
+    for k, dy in enumerate((2, 3, 1)):
         tok_copy(1 + k, b, y_block(dy)).wait_send()
         tok_copy(4 + k, b_z, y_block(dy)).wait_send()
 
@@ -378,7 +394,14 @@
         for stage in range(4):
             gather_copy(u, stage).wait_send()
 
-        @pl.when((u // 2 != 3) & (u // 2 != 7))
+        q = lax.rem(u // 2, 4)
+
+        @pl.when(q == 0)
+        def _():
+            for side in range(2):
+                relay_copy(u, side).wait_send()
+
+        @pl.when((q == 1) | (q == 2))
         def _():
             term_copy(u).wait_send()
 
@@ -427,8 +450,8 @@
             dma((4, UNITS)),
             dma((4, UNITS)),
             dma((4, UNITS)),
-            dma((UNITS,)),
-            dma((UNITS,)),
+            dma((2, UNITS)),
+            dma((2, UNITS)),
             dma((2,)),
             dma((2,)),
         ],

time: 113 us -> 119 us (1.053); the launches traced: 113 us -> 117 us
  Pallas kernels: 112 us -> 115 us
    pallas_call x1, Pallas kernels: 112 us -> 115 us  [per_device(): pl.pallas_call(kernel, out_shape=jax.ShapeDtypeStruct(tokens.shape, bf16)...]
where the time goes in v2:
time: 119 us; the launch traced here: 117 us
  Pallas kernels  115 us (97%)
  local copies, waits for them, and re-layouts  1.67 us (1%)
    pallas_call x1, Pallas kernels, per_device(): pl.pallas_call(kernel, out_shape=jax.ShapeDtypeStruct(tokens.shape, bf16)...  115 us

profile of v2, /device:TPU:8, one launch (start us, length us, event | category | flops | bytes accessed | tf_op | source)
XLA Modules:
  0.0 116.7 jit_solution(12341870372405061573)
XLA Ops:
  0.0 115.0 %shard_map.55 = bf16[512,256]{1,0:T(8,128)(2,1)} custom-call(f32[2,8]{1,0:T(2,128)} %gates_ref.1, bf16[512,256]{1,0:T(8,128)(2,1)} %tokens_ref.1, bf16[8,256,896]{2,1,0:T(8,128)(2,1)} %wg_ref.1, bf16[8,256,896]{2,1,0:T(8,128)(2,1)} %wu_ref.1, bf16[8,896,256]{2,1,0:T(8,128)(2,1)} %wd_ref.1), custom_call_target="tpu_custom_call" | custom-call | flops 17179869184 | bytes 12582912 | tf_op jit(solution)/shard_map/pallas_call | solution.py:421
  115.0 1.7 %copy.7 = bf16[512,256]{1,0:T(8,128)(2,1)} copy(bf16[512,256]{1,0:T(8,128)(2,1)} %shard_map.55) | data formatting | bytes 524288

commit v3 on v1

--- a/solution.py
+++ b/solution.py
@@ -13,7 +13,7 @@
 TILE = 256
 SLOTS = 4
 MESH = pl.DeviceIdType.MESH
-OFFSETS = (0, 1, 6, 9, 12, 15, 18, 22, 23)
+OFFSETS = (0, 1, 8, 12, 15, 18, 22, 27, 28)
 
 
 def kernel(

time: 113 us -> 116 us (1.027)
  Pallas kernels: 112 us -> 115 us
    pallas_call x1, Pallas kernels: 112 us -> 115 us  [per_device(): pl.pallas_call(kernel, out_shape=jax.ShapeDtypeStruct(tokens.shape, bf16)...]
where the time goes in v3:
time: 116 us
  Pallas kernels  115 us (99%)
  local copies, waits for them, and re-layouts  1.67 us (1%)
    pallas_call x1, Pallas kernels, per_device(): pl.pallas_call(kernel, out_shape=jax.ShapeDtypeStruct(tokens.shape, bf16)...  115 us

profile of v3, /device:TPU:8, one launch (start us, length us, event | category | flops | bytes accessed | tf_op | source)
XLA Modules:
  0.0 116.2 jit_solution(1841262540933079006)
XLA Ops:
  0.0 114.5 %shard_map.55 = bf16[512,256]{1,0:T(8,128)(2,1)} custom-call(f32[2,8]{1,0:T(2,128)} %gates_ref.1, bf16[512,256]{1,0:T(8,128)(2,1)} %tokens_ref.1, bf16[8,256,896]{2,1,0:T(8,128)(2,1)} %wg_ref.1, bf16[8,256,896]{2,1,0:T(8,128)(2,1)} %wu_ref.1, bf16[8,896,256]{2,1,0:T(8,128)(2,1)} %wd_ref.1), custom_call_target="tpu_custom_call" | custom-call | flops 17179869184 | bytes 12582912 | tf_op jit(solution)/shard_map/pallas_call | solution.py:398
  114.5 1.7 %copy.7 = bf16[512,256]{1,0:T(8,128)(2,1)} copy(bf16[512,256]{1,0:T(8,128)(2,1)} %shard_map.55) | data formatting | bytes 524288
